TPU v7x, 32 devices: a whole 2x2x4 slice. The times are simulated.
32 devices in a mesh: obs: 4 (over x, core), par: 8 (over z, y).
Axes of the slice: x: 2, y: 2, z: 4, core: 2. Of those that a mesh axis runs over, the one named last changes fastest.
Arguments:
- jacobian: bfloat16 [768, 16384], P(('obs', 'par')), may hold values from -0.21875 to 0.21875
- obs_weights: float32 [768], replicated, may hold values from 0.1 to 10
- time_to_obs: int32 [768], P(('obs', 'par')), may hold values from 0 to 767, each once
Outputs:
- normal_matrix: float32 [16384, 16384], P('obs', 'par')
Inputs may be any that keep to these rules, and one draw needn't show every extreme that they name: `time_to_obs`: each observation index appears exactly once.
All inputs are finite; a program needn't handle non-finite values.
Results may differ from a plain program's by a relative error of at most 0.0039.
Values may be sent and summed in bfloat16 or wider, within the bound.
A program may use at most 128 MiB of HBM per device.

v0:
```python
import jax
import jax.numpy as jnp
from jax import lax
from jax.sharding import PartitionSpec as P


def on_device(jacobian, obs_weights, time_to_obs):
    rows_here = jacobian.shape[0]
    param_count = jacobian.shape[1]
    obs_count = lax.axis_size("obs")
    par_count = lax.axis_size("par")
    indices = jnp.arange(obs_weights.shape[0], dtype=jnp.int32)
    picked = jnp.sum(
        jnp.where(time_to_obs[:, None] == indices[None, :], obs_weights[None, :], 0.0), axis=1
    )
    scaled = (jnp.sqrt(picked)[:, None] * jacobian.astype(jnp.float32)).astype(jnp.bfloat16)
    lifted = scaled.reshape(1, rows_here, param_count)
    blocks = lax.all_to_all(lifted, "obs", split_axis=2, concat_axis=0, tiled=True)
    col_width = param_count // par_count
    columns = lax.all_to_all(lifted, "par", split_axis=2, concat_axis=0, tiled=True)
    columns = lax.all_gather(columns, "obs", axis=0, tiled=True)
    columns = columns.reshape(obs_count, par_count * rows_here, col_width)
    panels = lax.all_gather(blocks, "par", axis=1, tiled=True)
    return jnp.einsum("arc,ard->cd", panels, columns, preferred_element_type=jnp.float32)


def solution(mesh):
    placed = (P(("obs", "par"), None), P(), P(("obs", "par")))
    return jax.shard_map(
        on_device, mesh=mesh, in_specs=placed, out_specs=P("obs", "par"), check_vma=False
    )
```

profile of v0, /device:TPU:0, one launch (start us, length us, event | category | flops | bytes accessed | tf_op | source)
XLA Modules:
  0.0 442.1 jit_solution(2540939693996147884)
XLA Ops:
  6.5 0.0 all-gather.7.cloned.1.call-start
  6.5 0.9 select_reduce_fusion
  7.4 1.3 fusion.1
  8.8 12.5 %copy.17 = bf16[1,24,16384]{1,0,2:T(2,128)(2,1)} copy(bf16[1,24,16384]{2,1,0:T(8,128)(2,1)S(1)} %fusion.1) | data formatting | bytes 1572864 | tf_op jit(solution)/shard_map/reshape | solution.py:17
  21.3 0.6 broadcast.2
  21.9 90.7 %reduce = bf16[16384,24]{1,0:T(8,128)(2,1)} reduce(bf16[16384,1,24]{2,1,0:T(2,128)(2,1)} %bitcast.28, bf16[]{:T(256)} %broadcast.2), dimensions={1}, to_apply=%bitcast.20.reduce_sub_computation | reduce | bytes 1572866
  112.6 6.6 %reshape.17 = bf16[8,2,24576]{2,1,0:T(2,128)(2,1)S(1)} reshape(bf16[16384,24]{1,0:T(8,128)(2,1)} %reduce) | data formatting | bytes 1572864
  119.2 27.2 %all_to_all.36 = bf16[8,2,24576]{2,1,0:T(2,128)(2,1)S(1)} all-to-all(bf16[8,2,24576]{2,1,0:T(2,128)(2,1)S(1)} %reshape.17), channel_id=1, replica_groups=mesh['obs'=4,'par'=8] {'par'}, dimensions={0} | all-to-all | bytes 1572864 | tf_op jit(solution)/shard_map/all_to_all | solution.py:20
  146.5 12.0 %reshape.18 = bf16[16384,1,24]{2,1,0:T(2,128)(2,1)} reshape(bf16[8,2,24576]{2,1,0:T(2,128)(2,1)S(1)} %all_to_all.36) | data formatting | bytes 1572864
  158.5 15.2 %copy.21 = bf16[1,24,16384]{2,1,0:T(8,128)(2,1)S(1)} copy(bf16[1,24,16384]{1,0,2:T(2,128)(2,1)} %bitcast.30) | data formatting | bytes 1572864 | tf_op jit(solution)/shard_map/all_to_all | solution.py:20
  173.7 0.4 copy.24
  174.1 0.1 bitcast_bitcast_fusion
  174.2 1.3 copy.22
  175.5 0.0 all-gather.7.cloned.1.call-update
  175.5 0.2 all-gather.5.cloned.1.call-start
  175.8 90.7 %reduce.1 = bf16[16384,24]{1,0:T(8,128)(2,1)} reduce(bf16[16384,1,24]{2,1,0:T(2,128)(2,1)} %bitcast.29, bf16[]{:T(256)} %broadcast.2), dimensions={1}, to_apply=%bitcast.22.reduce_sub_computation | reduce | bytes 1572866
  266.5 6.6 %reshape.19 = bf16[4,2,49152]{2,1,0:T(2,128)(2,1)S(1)} reshape(bf16[16384,24]{1,0:T(8,128)(2,1)} %reduce.1) | data formatting | bytes 1572864
  273.1 14.2 %all_to_all.37 = bf16[4,2,49152]{2,1,0:T(2,128)(2,1)S(1)} all-to-all(bf16[4,2,49152]{2,1,0:T(2,128)(2,1)S(1)} %reshape.19), channel_id=1, replica_groups=mesh['obs'=4,'par'=8] {'obs'}, dimensions={0} | all-to-all | bytes 1572864 | tf_op jit(solution)/shard_map/all_to_all | solution.py:18
  287.3 12.0 %reshape.20 = bf16[16384,1,24]{2,1,0:T(2,128)(2,1)} reshape(bf16[4,2,49152]{2,1,0:T(2,128)(2,1)S(1)} %all_to_all.37) | data formatting | bytes 1572864
  299.3 15.2 %copy.18 = bf16[1,24,16384]{2,1,0:T(8,128)(2,1)S(1)} copy(bf16[1,24,16384]{1,0,2:T(2,128)(2,1)} %bitcast.31) | data formatting | bytes 1572864 | tf_op jit(solution)/shard_map/all_to_all | solution.py:18
  314.5 0.9 copy.26
  315.4 0.0 all-gather.5.cloned.1.call-update
  315.4 0.0 all-gather.7.cloned.1.call-done
  315.4 97.2 %all-gather.5.cloned.1.call-done = bf16[4,1,192,4096]{3,2,0,1:T(8,128)(2,1)} async-done(((bf16[4,1,24,4096]{3,2,0,1:T(8,128)(2,1)}), bf16[4,1,192,4096]{3,2,0,1:T(8,128)(2,1)}) %all-gather.5.cloned.1.call-update) | async-done | bytes 6291472 | tf_op jit(solution)/shard_map/all_gather | solution.py:23
  412.7 22.5 %convolution_bitcast_fusion = f32[4096,2048]{1,0:T(8,128)} fusion(bf16[4,192,2048]{2,1,0:T(8,128)(2,1)} %bitcast.36, bf16[4,1,192,4096]{3,2,0,1:T(8,128)(2,1)} %all-gather.5.cloned.1.call-done), kind=kOutput, calls=%fused_computation | convolution fusion | flops 12884901888 | bytes 42991616 | tf_op jit(solution)/shard_map/arc,ard->cd/dot_general | solution.py:24
  (1 shorter events, 0.0 us)
Async XLA Ops:
  6.5 308.9 %all-gather.7.cloned.1.call-start = ((), (), s32[]{:S(2)}) async-start(), calls=%async_computation.3 | async-start | bytes 3932160 | tf_op jit(solution)/shard_map/all_gather | solution.py:21
  175.5 237.1 %all-gather.5.cloned.1.call-start = ((), (), s32[]{:S(2)}) async-start(), calls=%async_computation.2 | async-start | bytes 7077888 | tf_op jit(solution)/shard_map/all_gather | solution.py:23
Sparse Core Ops, SparseCore 0:
  175.7 27.5 all-gather.6
  315.5 97.0 all-gather.4
where the time goes:
time: 443 us; the launch traced here: 442 us
  other arithmetic  184 us (42%)
  waiting for transfers between devices  97.3 us (22%)
  local copies, waits for them, and re-layouts  83.5 us (19%)
  blocking collectives  41.4 us (9%)
  matrix products  22.5 us (5%)
  between operations  13.5 us (3%)
    unnamed x2, other arithmetic  181 us
    all_gather x1, waiting for transfers between devices, on_device(): panels = lax.all_gather(blocks, 'par', axis=1, tiled=True)  97.2 us
    unnamed x6, local copies, waits for them, and re-layouts  38.3 us
    all_to_all x1, blocking collectives, on_device(): lax.all_to_all(lifted, 'par', split_axis=2, concat_axis=0, tiled=True)  27.2 us
    dot_general x1, matrix products, on_device(): jnp.einsum('arc,ard->cd', panels, columns, preferred_element_type=jnp.flo...  22.5 us
    all_to_all x3, local copies, waits for them, and re-layouts, on_device(): lax.all_to_all(lifted, 'par', split_axis=2, concat_axis=0, tiled=True)  16.6 us
    all_to_all x2, local copies, waits for them, and re-layouts, on_device(): lax.all_to_all(lifted, 'obs', split_axis=2, concat_axis=0, tiled=True)  16.1 us
    all_to_all x1, blocking collectives, on_device(): lax.all_to_all(lifted, 'obs', split_axis=2, concat_axis=0, tiled=True)  14.2 us
  transfers between devices with their start and end apart: 2, of which 1 were waited for; matrix products, arithmetic and copies ran while one was open for 28% of the time, Pallas kernels for 0%

commit v1 on v0

v1 whole, which is shorter than its diff:
```python
import functools
import itertools

import jax
import jax.numpy as jnp
from jax import lax
from jax.experimental import pallas as pl
from jax.experimental.pallas import tpu as pltpu
from jax.sharding import PartitionSpec as P

MESH = pl.DeviceIdType.MESH
LAG = 12


def grid_of(par_count):
    return {8: (4, 2), 32: (4, 4, 2)}.get(par_count, (par_count,))


def schedule(dims):
    spans = [(0, 1) if n == 2 else tuple(range(1 - n, n)) for n in dims]
    steps = [(off, turn) for off in itertools.product(*spans) for turn in range(4)]
    late = (0.0, 0.0, 0.5, 0.5)
    return sorted(
        steps,
        key=lambda s: (sum(abs(o) for o in s[0]) + late[s[1]], s[1], [abs(o) for o in reversed(s[0])], s[0]),
    )


def guarded(conds, action):
    if not conds:
        action()
        return
    both = conds[0]
    for cond in conds[1:]:
        both = jnp.logical_and(both, cond)
    pl.when(both)(action)


def gather_kernel(dims, late_first, scaled, panel, cols, own_sem, recv, col_recv, obs_send, par_send, col_send):
    a, b = lax.axis_index("obs"), lax.axis_index("par")
    core, chip = a % 2, a // 2
    quarter, width = panel.shape[2], cols.shape[2]
    per = quarter // width
    is_owner = a == b // per
    on_owner_chip = chip == (b // per) // 2
    strides, where = [], []
    stride = 1
    for n in reversed(dims):
        strides.insert(0, stride)
        where.insert(0, (b // stride) % n)
        stride *= n
    rank = len(dims)

    def obs_of(turn):
        return 2 * ((chip + turn // 2) % 2) + (core + turn % 2) % 2

    def hop(dim, sign):
        n, at = dims[dim], where[dim]
        if n == 2:
            return b + (1 - 2 * at) * strides[dim], []
        return b + sign * strides[dim], [at < n - 1 if sign > 0 else at > 0]

    def remote(src, dst, send_sem, recv_sem, obs, par):
        return pltpu.make_async_remote_copy(
            src_ref=src, dst_ref=dst, send_sem=send_sem, recv_sem=recv_sem,
            device_id=(obs, par), device_id_type=MESH,
        )

    def here(step):
        conds = []
        for dim, off in enumerate(step[0]):
            if dims[dim] > 2 and off:
                conds.append(where[dim] + off < dims[dim] if off > 0 else where[dim] + off >= 0)
        return conds

    def slot_of(step):
        origin = b
        for dim, off in enumerate(step[0]):
            if off:
                origin = origin + ((1 - 2 * where[dim]) if dims[dim] == 2 else off) * strides[dim]
        source = obs_of(step[1])
        return 4 * origin + source, source

    def is_own(step):
        return step[1] == 0 and not any(step[0])

    def view(step, slot):
        if is_own(step):
            return scaled.at[:, pl.ds(pl.multiple_of(a * quarter, 128), quarter)]
        return panel.at[slot]

    def col_view(step, slot):
        if is_own(step):
            return scaled.at[:, pl.ds(pl.multiple_of(b * width, 128), width)]
        return panel.at[slot, :, pl.ds(pl.multiple_of((b % per) * width, 128), width)]

    def forwards(step):
        order = list(range(rank))
        if step[1] == 3 and late_first:
            order = order[::-1]
        moved = [i for i in range(rank) if step[0][order[i]]]
        last = moved[-1] if moved else -1
        out = []
        for i in range(max(last, 0), rank):
            dim = order[i]
            if i == last:
                if dims[dim] > 2:
                    out.append((dim, -1 if step[0][dim] > 0 else 1))
            elif dims[dim] == 2:
                out.append((dim, 1))
            else:
                out += [(dim, 1), (dim, -1)]
        return out

    def par_copy(step, slot, dim, sign):
        return remote(
            view(step, slot), panel.at[slot], par_send.at[2 * dim + (sign > 0), slot], recv.at[slot],
            a, hop(dim, sign)[0],
        )

    def col_copies(step, slot, source):
        src = col_view(step, slot)
        return (
            remote(src, cols.at[slot], col_send.at[0, slot], col_recv.at[slot], 2 * chip + 1 - core, b),
            remote(src, cols.at[slot], col_send.at[1, slot], col_recv.at[slot], 2 * (1 - chip) + source % 2, b),
        )

    def relay(slot):
        return remote(
            cols.at[slot], cols.at[slot], col_send.at[2, slot], col_recv.at[slot], 2 * chip + 1 - core, b
        )

    def arrive(step):
        def run():
            slot, source = slot_of(step)
            if not is_own(step):
                pltpu.make_async_copy(panel.at[slot], panel.at[slot], recv.at[slot]).wait()
            for dim, sign in forwards(step):
                guarded(hop(dim, sign)[1], lambda: par_copy(step, slot, dim, sign).start())

            @pl.when(is_owner)
            def _():
                for copy in col_copies(step, slot, source):
                    copy.start()
                pltpu.make_async_copy(col_view(step, slot), cols.at[slot], col_recv.at[slot]).start()

        guarded(here(step), run)

    def take_cols(step):
        def run():
            slot, source = slot_of(step)
            pltpu.make_async_copy(cols.at[slot], cols.at[slot], col_recv.at[slot]).wait()
            pl.when(jnp.logical_and(jnp.logical_not(on_owner_chip), core == source % 2))(
                lambda: relay(slot).start()
            )

        guarded(here(step), run)

    def finish(step):
        def run():
            slot, source = slot_of(step)
            for dim, sign in forwards(step):
                guarded(hop(dim, sign)[1], lambda: par_copy(step, slot, dim, sign).wait_send())

            @pl.when(is_owner)
            def _():
                for copy in col_copies(step, slot, source):
                    copy.wait_send()

            pl.when(jnp.logical_and(jnp.logical_not(on_owner_chip), core == source % 2))(
                lambda: relay(slot).wait_send()
            )

        guarded(here(step), run)

    barrier = pltpu.get_barrier_semaphore()
    mates = [(obs_of(turn), b, []) for turn in (1, 2, 3)]
    for dim in range(rank):
        for sign in (1,) if dims[dim] == 2 else (1, -1):
            mates.append((a, *hop(dim, sign)))
    for obs, par, conds in mates:
        guarded(conds, lambda: pl.semaphore_signal(barrier, inc=1, device_id=(obs, par), device_id_type=MESH))
    count = sum(not conds for _, _, conds in mates)
    for _, _, conds in mates:
        for cond in conds:
            count = count + cond.astype(jnp.int32)
    pl.semaphore_wait(barrier, count)

    mine = 4 * b + a
    to_obs = []
    for turn in (2, 3, 1):
        obs = obs_of(turn)
        to_obs.append(remote(
            scaled.at[:, pl.ds(pl.multiple_of(obs * quarter, 128), quarter)], panel.at[mine],
            obs_send.at[turn], recv.at[mine], obs, b,
        ))
        to_obs[-1].start()
    keep = pltpu.make_async_copy(
        scaled.at[:, pl.ds(pl.multiple_of(a * quarter, 128), quarter)], panel.at[mine], own_sem.at[0]
    )
    keep.start()
    steps = schedule(dims)
    for i, step in enumerate(steps):
        arrive(step)
        if i >= LAG:
            take_cols(steps[i - LAG])
    for step in steps[-LAG:]:
        take_cols(step)
    keep.wait()
    for copy in to_obs:
        copy.wait_send()
    for step in steps:
        finish(step)


def on_device(obs_count, par_count, jacobian, obs_weights, time_to_obs):
    rows_here, param_count = jacobian.shape
    indices = jnp.arange(obs_weights.shape[0], dtype=jnp.int32)
    picked = jnp.sum(
        jnp.where(time_to_obs[:, None] == indices[None, :], obs_weights[None, :], 0.0), axis=1
    )
    scaled = (jnp.sqrt(picked)[:, None] * jacobian.astype(jnp.float32)).astype(jnp.bfloat16)
    dims = grid_of(par_count)
    slots = obs_count * par_count
    quarter, width = param_count // obs_count, param_count // par_count
    dma = pltpu.SemaphoreType.DMA
    panel, cols = pl.pallas_call(
        functools.partial(gather_kernel, dims, dims == (4, 2)),
        out_shape=(
            jax.ShapeDtypeStruct((slots, rows_here, quarter), jnp.bfloat16),
            jax.ShapeDtypeStruct((slots, rows_here, width), jnp.bfloat16),
        ),
        in_specs=[pl.BlockSpec(memory_space=pl.ANY)],
        out_specs=(pl.BlockSpec(memory_space=pl.ANY),) * 2,
        scratch_shapes=[
            dma((1,)), dma((slots,)), dma((slots,)), dma((4,)), dma((2 * len(dims), slots)), dma((3, slots)),
        ],
        compiler_params=pltpu.CompilerParams(collective_id=0, has_side_effects=True),
        name="gather",
    )(scaled)
    return jnp.einsum("src,srd->cd", panel, cols, preferred_element_type=jnp.float32)


def solution(mesh):
    placed = (P(("obs", "par"), None), P(), P(("obs", "par")))
    return jax.shard_map(
        functools.partial(on_device, mesh.shape["obs"], mesh.shape["par"]),
        mesh=mesh, in_specs=placed, out_specs=P("obs", "par"), check_vma=False,
    )
```

time: 443 us -> 134 us (0.30)
  other arithmetic: 184 us -> 3.09 us
  Pallas kernels: 0 us -> 108 us
  waiting for transfers between devices: 97.3 us -> 0 us
  local copies, waits for them, and re-layouts: 83.5 us -> 0.01 us
  blocking collectives: 41.4 us -> 0 us
  between operations: 13.5 us -> 0.01 us
    unnamed x2 -> x0, other arithmetic: 181 us -> none
    pallas_call x0 -> x1, Pallas kernels: none -> 108 us  [on_device(): pl.pallas_call(functools.partial(gather_kernel, dims, dims == (4, 2)), ou...]
    all_gather x2 -> x0, waiting for transfers between devices: 97.3 us -> none  [the longest x1 97.2 us: on_device(): panels = lax.all_gather(blocks, 'par', axis=1, tiled=True)]
    all_to_all x2 -> x0, blocking collectives: 41.4 us -> none  [the longest x1 27.2 us: on_device(): lax.all_to_all(lifted, 'par', split_axis=2, concat_axis=0, tiled=True)]
    unnamed x6 -> x0, local copies, waits for them, and re-layouts: 38.3 us -> none
    all_to_all x5 -> x0, local copies, waits for them, and re-layouts: 32.7 us -> none  [the longest x3 16.6 us: on_device(): lax.all_to_all(lifted, 'par', split_axis=2, concat_axis=0, tiled=True)]
    reshape x1 -> x0, local copies, waits for them, and re-layouts: 12.5 us -> none  [on_device(): lifted = scaled.reshape(1, rows_here, param_count)]
  transfers between devices with their start and end apart: 2 -> 0, of which waited for: 1 -> 0; matrix products, arithmetic and copies ran while one was open for 28% -> 0% of each run, Pallas kernels for 0% -> 0%
where the time goes in v1:
time: 134 us
  Pallas kernels  108 us (81%)
  matrix products  22.5 us (17%)
  other arithmetic  3.09 us (2%)
    pallas_call x1, Pallas kernels, on_device(): pl.pallas_call(functools.partial(gather_kernel, dims, dims == (4, 2)), ou...  108 us
    dot_general x1, matrix products, on_device(): jnp.einsum('src,srd->cd', panel, cols, preferred_element_type=jnp.float32)  22.5 us

profile of v1, /device:TPU:0, one launch (start us, length us, event | category | flops | bytes accessed | tf_op | source)
XLA Modules:
  0.0 134.0 jit_solution(8490449977417182876)
XLA Ops:
  0.0 0.9 select_reduce_fusion
  0.9 2.2 %multiply_convert_fusion.scaled = bf16[24,16384]{1,0:T(8,128)(2,1)} fusion(bf16[24,16384]{1,0:T(8,128)(2,1)} %param.3, f32[24]{0:T(128)S(1)} %sqrt.7), kind=kLoop, calls=%fused_computation.1 | loop fusion | flops 1179648 | bytes 1572960 | tf_op jit(solution)/shard_map/convert_element_type | solution.py:222
  3.1 108.4 %gather.1 = (bf16[32,24,4096]{2,1,0:T(8,128)(2,1)}, bf16[32,24,2048]{2,1,0:T(8,128)(2,1)}) custom-call(bf16[24,16384]{1,0:T(8,128)(2,1)} %multiply_convert_fusion.scaled), custom_call_target="tpu_custom_call" | custom-call | tf_op jit(solution)/shard_map/gather/pallas_call | solution.py:227
  111.5 22.5 %convolution_bitcast_fusion = f32[4096,2048]{1,0:T(8,128)} fusion(bf16[32,24,4096]{2,1,0:T(8,128)(2,1)} %get-tuple-element.7, bf16[32,24,2048]{2,1,0:T(8,128)(2,1)} %get-tuple-element.8), kind=kOutput, calls=%fused_computation | convolution fusion | flops 12884901888 | bytes 42991616 | tf_op jit(solution)/shard_map/src,srd->cd/dot_general | solution.py:241
  (1 shorter events, 0.0 us)

commit v2 on v1

--- a/solution.py
+++ b/solution.py
@@ -16,14 +16,48 @@
     return {8: (4, 2), 32: (4, 4, 2)}.get(par_count, (par_count,))
 
 
-def schedule(dims):
+def forwards(dims, late_first, step):
+    rank = len(dims)
+    order = list(range(rank))
+    if step[1] == 3 and late_first:
+        order = order[::-1]
+    moved = [i for i in range(rank) if step[0][order[i]]]
+    last = moved[-1] if moved else -1
+    out = []
+    for i in range(max(last, 0), rank):
+        dim = order[i]
+        if i == last:
+            if dims[dim] > 2:
+                out.append((dim, -1 if step[0][dim] > 0 else 1))
+        elif dims[dim] == 2:
+            out.append((dim, 1))
+        else:
+            out += [(dim, 1), (dim, -1)]
+    return out
+
+
+def schedule(dims, late_first):
     spans = [(0, 1) if n == 2 else tuple(range(1 - n, n)) for n in dims]
     steps = [(off, turn) for off in itertools.product(*spans) for turn in range(4)]
-    late = (0.0, 0.0, 0.5, 0.5)
-    return sorted(
-        steps,
-        key=lambda s: (sum(abs(o) for o in s[0]) + late[s[1]], s[1], [abs(o) for o in reversed(s[0])], s[0]),
-    )
+
+    def due(step):
+        off, turn = step
+        away = sum(abs(o) for o in off) + 0.5 * (turn // 2)
+        away += 0.75 * (off[-1] != 0)
+        return away, turn, [abs(o) for o in reversed(off)], off
+
+    return sorted(steps, key=due)
+
+
+def sends_at(dims, late_first, place):
+    sent = {}
+    for step in schedule(dims, late_first):
+        if all(0 <= place[dim] + step[0][dim] < dims[dim] for dim in place):
+            for dim, sign in forwards(dims, late_first, step):
+                if dim not in place or 0 <= place[dim] + sign < dims[dim]:
+                    way = 2 * dim + (sign > 0)
+                    sent[way] = sent.get(way, 0) + 1
+    return sent
 
 
 def guarded(conds, action):
@@ -94,84 +128,71 @@
             return scaled.at[:, pl.ds(pl.multiple_of(b * width, 128), width)]
         return panel.at[slot, :, pl.ds(pl.multiple_of((b % per) * width, 128), width)]
 
-    def forwards(step):
-        order = list(range(rank))
-        if step[1] == 3 and late_first:
-            order = order[::-1]
-        moved = [i for i in range(rank) if step[0][order[i]]]
-        last = moved[-1] if moved else -1
-        out = []
-        for i in range(max(last, 0), rank):
-            dim = order[i]
-            if i == last:
-                if dims[dim] > 2:
-                    out.append((dim, -1 if step[0][dim] > 0 else 1))
-            elif dims[dim] == 2:
-                out.append((dim, 1))
-            else:
-                out += [(dim, 1), (dim, -1)]
-        return out
-
     def par_copy(step, slot, dim, sign):
         return remote(
-            view(step, slot), panel.at[slot], par_send.at[2 * dim + (sign > 0), slot], recv.at[slot],
+            view(step, slot), panel.at[slot], par_send.at[2 * dim + (sign > 0)], recv.at[slot],
             a, hop(dim, sign)[0],
         )
 
     def col_copies(step, slot, source):
         src = col_view(step, slot)
         return (
-            remote(src, cols.at[slot], col_send.at[0, slot], col_recv.at[slot], 2 * chip + 1 - core, b),
-            remote(src, cols.at[slot], col_send.at[1, slot], col_recv.at[slot], 2 * (1 - chip) + source % 2, b),
+            remote(src, cols.at[slot], col_send.at[0], col_recv.at[slot], 2 * chip + 1 - core, b),
+            remote(src, cols.at[slot], col_send.at[1], col_recv.at[slot], 2 * (1 - chip) + source % 2, b),
         )
 
     def relay(slot):
         return remote(
-            cols.at[slot], cols.at[slot], col_send.at[2, slot], col_recv.at[slot], 2 * chip + 1 - core, b
-        )
+            cols.at[slot], cols.at[slot], col_send.at[2], col_recv.at[slot], 2 * chip + 1 - core, b
+        )
+
+    def drain(ref, sem):
+        pltpu.make_async_copy(ref, ref, sem).wait()
 
     def arrive(step):
         def run():
             slot, source = slot_of(step)
             if not is_own(step):
-                pltpu.make_async_copy(panel.at[slot], panel.at[slot], recv.at[slot]).wait()
-            for dim, sign in forwards(step):
+                drain(panel.at[slot], recv.at[slot])
+            for dim, sign in forwards(dims, late_first, step):
                 guarded(hop(dim, sign)[1], lambda: par_copy(step, slot, dim, sign).start())
 
             @pl.when(is_owner)
             def _():
                 for copy in col_copies(step, slot, source):
                     copy.start()
-                pltpu.make_async_copy(col_view(step, slot), cols.at[slot], col_recv.at[slot]).start()
 
         guarded(here(step), run)
 
     def take_cols(step):
         def run():
             slot, source = slot_of(step)
-            pltpu.make_async_copy(cols.at[slot], cols.at[slot], col_recv.at[slot]).wait()
+            drain(cols.at[slot], col_recv.at[slot])
             pl.when(jnp.logical_and(jnp.logical_not(on_owner_chip), core == source % 2))(
                 lambda: relay(slot).start()
             )
 
-        guarded(here(step), run)
-
-    def finish(step):
-        def run():
-            slot, source = slot_of(step)
-            for dim, sign in forwards(step):
-                guarded(hop(dim, sign)[1], lambda: par_copy(step, slot, dim, sign).wait_send())
-
-            @pl.when(is_owner)
-            def _():
-                for copy in col_copies(step, slot, source):
-                    copy.wait_send()
-
-            pl.when(jnp.logical_and(jnp.logical_not(on_owner_chip), core == source % 2))(
-                lambda: relay(slot).wait_send()
-            )
-
-        guarded(here(step), run)
+        guarded([jnp.logical_not(is_owner), *here(step)], run)
+
+    def finish():
+        long = [dim for dim in range(rank) if dims[dim] > 2]
+        for place in itertools.product(*(range(dims[dim]) for dim in long)):
+            sent = sends_at(dims, late_first, dict(zip(long, place)))
+
+            def run():
+                for way in sorted(sent):
+                    drain(panel.at[pl.ds(0, sent[way])], par_send.at[way])
+
+            guarded([where[dim] == at for dim, at in zip(long, place)], run)
+
+        @pl.when(is_owner)
+        def _():
+            drain(cols, col_send.at[0])
+            drain(cols, col_send.at[1])
+
+        pl.when(jnp.logical_not(on_owner_chip))(
+            lambda: drain(cols.at[pl.ds(0, cols.shape[0] // 2)], col_send.at[2])
+        )
 
     barrier = pltpu.get_barrier_semaphore()
     mates = [(obs_of(turn), b, []) for turn in (1, 2, 3)]
@@ -199,18 +220,41 @@
         scaled.at[:, pl.ds(pl.multiple_of(a * quarter, 128), quarter)], panel.at[mine], own_sem.at[0]
     )
     keep.start()
-    steps = schedule(dims)
+    steps = schedule(dims, late_first)
+    lag = LAG if rank < 3 else len(steps)
     for i, step in enumerate(steps):
         arrive(step)
-        if i >= LAG:
-            take_cols(steps[i - LAG])
-    for step in steps[-LAG:]:
+        if i >= lag:
+            take_cols(steps[i - lag])
+    for step in steps[-lag:]:
         take_cols(step)
     keep.wait()
     for copy in to_obs:
         copy.wait_send()
-    for step in steps:
-        finish(step)
+    finish()
+
+
+def product_kernel(per, panel, panel_all, cols, out, right, sem):
+    a, b = lax.axis_index("obs"), lax.axis_index("par")
+    width = right.shape[1]
+
+    @pl.when(pl.program_id(0) == 0)
+    def _():
+        own = pl.ds(pl.multiple_of((b % per) * width, 128), width)
+
+        @pl.when(a == b // per)
+        def _():
+            pltpu.make_async_copy(panel_all.at[:, own], right, sem).start()
+
+        @pl.when(a != b // per)
+        def _():
+            pltpu.make_async_copy(cols, right, sem).start()
+
+        pltpu.make_async_copy(cols, right, sem).wait()
+
+    out[...] = lax.dot_general(
+        panel[...], right[...], (((0,), (0,)), ((), ())), preferred_element_type=jnp.float32
+    )
 
 
 def on_device(obs_count, par_count, jacobian, obs_weights, time_to_obs):
@@ -233,12 +277,28 @@
         in_specs=[pl.BlockSpec(memory_space=pl.ANY)],
         out_specs=(pl.BlockSpec(memory_space=pl.ANY),) * 2,
         scratch_shapes=[
-            dma((1,)), dma((slots,)), dma((slots,)), dma((4,)), dma((2 * len(dims), slots)), dma((3, slots)),
+            dma((1,)), dma((slots,)), dma((slots,)), dma((4,)), dma((2 * len(dims),)), dma((3,)),
         ],
         compiler_params=pltpu.CompilerParams(collective_id=0, has_side_effects=True),
         name="gather",
     )(scaled)
-    return jnp.einsum("src,srd->cd", panel, cols, preferred_element_type=jnp.float32)
+    rows = slots * rows_here
+    panel, cols = panel.reshape(rows, quarter), cols.reshape(rows, width)
+    tile = 256
+    return pl.pallas_call(
+        functools.partial(product_kernel, quarter // width),
+        out_shape=jax.ShapeDtypeStruct((quarter, width), jnp.float32),
+        grid=(quarter // tile,),
+        in_specs=[
+            pl.BlockSpec((rows, tile), lambda i: (0, i)),
+            pl.BlockSpec(memory_space=pl.ANY),
+            pl.BlockSpec(memory_space=pl.ANY),
+        ],
+        out_specs=pl.BlockSpec((tile, width), lambda i: (i, 0)),
+        scratch_shapes=[pltpu.VMEM((rows, width), jnp.bfloat16), dma],
+        compiler_params=pltpu.CompilerParams(vmem_limit_bytes=48 * 2**20),
+        name="product",
+    )(panel, panel, cols)
 
 
 def solution(mesh):

time: 134 us -> 103 us (0.77); the launches traced: 134 us -> 101 us
  matrix products: 22.5 us -> 0 us
  Pallas kernels: 108 us -> 96.1 us
  local copies, waits for them, and re-layouts: 0.01 us -> 1.89 us
    pallas_call x1, Pallas kernels: 108 us -> 72.8 us  [on_device(): pl.pallas_call(functools.partial(gather_kernel, dims, dims == (4, 2)), ou...]
    pallas_call x0 -> x1, Pallas kernels: none -> 23.4 us  [on_device(): pl.pallas_call(functools.partial(product_kernel, quarter // width), out_s...]
    dot_general x1 -> x0, matrix products: 22.5 us -> none  [on_device(): jnp.einsum('src,srd->cd', panel, cols, preferred_element_type=jnp.float32)]
    unnamed x0 -> x2, local copies, waits for them, and re-layouts: none -> 1.88 us
where the time goes in v2:
time: 103 us; the launch traced here: 101 us
  Pallas kernels  96.1 us (93%)
  other arithmetic  3.09 us (3%)
  local copies, waits for them, and re-layouts  1.89 us (2%)
    pallas_call x1, Pallas kernels, on_device(): pl.pallas_call(functools.partial(gather_kernel, dims, dims == (4, 2)), ou...  72.8 us
    pallas_call x1, Pallas kernels, on_device(): pl.pallas_call(functools.partial(product_kernel, quarter // width), out_s...  23.4 us
    convert_element_type x1, other arithmetic, on_device(): (jnp.sqrt(picked)[:, None] * jacobian.astype(jnp.float32)).astype(jnp.bfl...  2.22 us

profile of v2, /device:TPU:0, one launch (start us, length us, event | category | flops | bytes accessed | tf_op | source)
XLA Modules:
  0.0 101.1 jit_solution(12593774038171523061)
XLA Ops:
  0.0 0.9 select_reduce_fusion
  0.9 2.2 %multiply_convert_fusion.scaled = bf16[24,16384]{1,0:T(8,128)(2,1)} fusion(bf16[24,16384]{1,0:T(8,128)(2,1)} %param.3, f32[24]{0:T(128)S(1)} %sqrt.7), kind=kLoop, calls=%fused_computation | loop fusion | flops 1179648 | bytes 1572960 | tf_op jit(solution)/shard_map/convert_element_type | solution.py:266
  3.1 72.8 %gather.1 = (bf16[32,24,4096]{2,1,0:T(8,128)(2,1)}, bf16[32,24,2048]{2,1,0:T(8,128)(2,1)}) custom-call(bf16[24,16384]{1,0:T(8,128)(2,1)} %multiply_convert_fusion.scaled), custom_call_target="tpu_custom_call" | custom-call | tf_op jit(solution)/shard_map/gather/pallas_call | solution.py:271
  75.9 0.0 copy-start
  75.9 1.9 %copy-done = bf16[32,24,2048]{2,1,0:T(8,128)(2,1)S(1)} copy-done((bf16[32,24,2048]{2,1,0:T(8,128)(2,1)S(1)}, bf16[32,24,2048]{2,1,0:T(8,128)(2,1)}, u32[]{:S(2)}) %copy-start) | copy-done | bytes 3145752
  77.8 23.4 %product.1 = f32[4096,2048]{1,0:T(8,128)} custom-call(bf16[768,4096]{1,0:T(8,128)(2,1)} %bitcast.3, bf16[768,4096]{1,0:T(8,128)(2,1)} %bitcast.4, bf16[768,2048]{1,0:T(8,128)(2,1)S(1)} %bitcast.2), custom_call_target="tpu_custom_call" | custom-call | tf_op jit(solution)/shard_map/product/pallas_call | solution.py:288
  (1 shorter events, 0.0 us)
Async XLA Ops:
  75.9 1.9 %copy-start = (bf16[32,24,2048]{2,1,0:T(8,128)(2,1)S(1)}, bf16[32,24,2048]{2,1,0:T(8,128)(2,1)}, u32[]{:S(2)}) copy-start(bf16[32,24,2048]{2,1,0:T(8,128)(2,1)} %get-tuple-element.8) | copy-start | bytes 9437188

commit v3 on v2

--- a/solution.py
+++ b/solution.py
@@ -284,7 +284,7 @@
     )(scaled)
     rows = slots * rows_here
     panel, cols = panel.reshape(rows, quarter), cols.reshape(rows, width)
-    tile = 256
+    tile = 512
     return pl.pallas_call(
         functools.partial(product_kernel, quarter // width),
         out_shape=jax.ShapeDtypeStruct((quarter, width), jnp.float32),
@@ -296,7 +296,7 @@
         ],
         out_specs=pl.BlockSpec((tile, width), lambda i: (i, 0)),
         scratch_shapes=[pltpu.VMEM((rows, width), jnp.bfloat16), dma],
-        compiler_params=pltpu.CompilerParams(vmem_limit_bytes=48 * 2**20),
+        compiler_params=pltpu.CompilerParams(vmem_limit_bytes=60 * 2**20, fuse_transposed_lhs_in_matmul=True),
         name="product",
     )(panel, panel, cols)
 

time: 103 us -> 109 us (1.058)
  the two profiles are of different devices: /device:TPU:0 before, /device:TPU:3 now
where the time goes in v3:
time: 109 us
  Pallas kernels  106 us (97%)
  other arithmetic  3.09 us (3%)
    pallas_call x1, Pallas kernels, on_device(): pl.pallas_call(functools.partial(gather_kernel, dims, dims == (4, 2)), ou...  75.1 us
    pallas_call x1, Pallas kernels, on_device(): pl.pallas_call(functools.partial(product_kernel, quarter // width), out_s...  30.6 us
    convert_element_type x1, other arithmetic, on_device(): (jnp.sqrt(picked)[:, None] * jacobian.astype(jnp.float32)).astype(jnp.bfl...  2.22 us

profile of v3, /device:TPU:3, one launch (start us, length us, event | category | flops | bytes accessed | tf_op | source)
XLA Modules:
  0.0 108.8 jit_solution(6352505030719126677)
XLA Ops:
  0.0 0.9 select_reduce_fusion
  0.9 2.2 %multiply_convert_fusion.scaled = bf16[24,16384]{1,0:T(8,128)(2,1)} fusion(bf16[24,16384]{1,0:T(8,128)(2,1)} %param.3, f32[24]{0:T(128)S(1)} %sqrt.7), kind=kLoop, calls=%fused_computation | loop fusion | flops 1179648 | bytes 1572960 | tf_op jit(solution)/shard_map/convert_element_type | solution.py:266
  3.1 75.1 %gather.1 = (bf16[32,24,4096]{2,1,0:T(8,128)(2,1)}, bf16[32,24,2048]{2,1,0:T(8,128)(2,1)}) custom-call(bf16[24,16384]{1,0:T(8,128)(2,1)} %multiply_convert_fusion.scaled), custom_call_target="tpu_custom_call" | custom-call | tf_op jit(solution)/shard_map/gather/pallas_call | solution.py:271
  78.2 30.6 %product.1 = f32[4096,2048]{1,0:T(8,128)} custom-call(bf16[768,4096]{1,0:T(8,128)(2,1)} %bitcast.2, bf16[768,4096]{1,0:T(8,128)(2,1)} %bitcast.3, bf16[768,2048]{1,0:T(8,128)(2,1)} %bitcast.4), custom_call_target="tpu_custom_call" | custom-call | tf_op jit(solution)/shard_map/product/pallas_call | solution.py:288
  (1 shorter events, 0.0 us)
